TPU v7x, 32 devices: a whole 2x2x4 slice. The times are simulated.
32 devices in a mesh: dp: 4 (over z), mp: 2 (over y), expert: 4 (over x, core).
Axes of the slice: x: 2, y: 2, z: 4, core: 2. Of those that a mesh axis runs over, the one named last changes fastest.
Arguments:
- attn_out: bfloat16 [1024, 2304], P('dp', 'mp'), may hold values from -6 to 6
- residual: float32 [1024, 2304], P(('dp', 'mp', 'expert'))
- proj_weight: bfloat16 [2304, 2304], P('mp'), may hold values from -0.125 to 0.125
- norm_gain: float32 [2304], replicated, may hold values from 0.1 to 1.9
- gate_weight: bfloat16 [8, 2304, 4096], P('mp', None, 'expert'), may hold values from -0.125 to 0.125
- up_weight: bfloat16 [8, 2304, 4096], P('mp', None, 'expert'), may hold values from -0.125 to 0.125
- down_weight: bfloat16 [8, 4096, 2304], P('mp', 'expert'), may hold values from -0.09375 to 0.09375
- routes: int32 [1024, 2], P(('dp', 'mp', 'expert')), may hold values from 0 to 7, as said below
- route_weights: float32 [1024, 2], P(('dp', 'mp', 'expert')), may hold values from 0.2 to 1
Outputs:
- mixed: float32 [1024, 2304], P(('dp', 'mp', 'expert'))
Inputs may be any that keep to these rules, and one draw needn't show every extreme that they name: `routes`: the two ids of a row differ. In the rows of each device (aligned blocks of 32 rows, in order) every expert is named by at most 16 rows; one expert, the same in all blocks, is named by exactly 16 rows in every block, and the other 48 names of a block are spread as evenly as possible over the other experts.
All inputs are finite; a program needn't handle non-finite values.
Results may differ from a plain program's by a relative error of at most 0.0015.
Values may be sent and summed in bfloat16 or wider, within the bound.
A program may use at most 128 MiB of HBM per device.

v0:
```python
import jax
import jax.numpy as jnp
from jax import lax
from jax.sharding import PartitionSpec as P

EXPERTS = 8
MOST = 16


EPSILON = 1e-06


def body(
    attn_out,
    residual,
    proj_weight,
    norm_gain,
    gate_weight,
    up_weight,
    down_weight,
    routes,
    route_weights,
):
    model_parts = lax.axis_size("mp")
    unit_parts = lax.axis_size("expert")
    row_count = residual.shape[0]
    features = residual.shape[1]
    local_experts = gate_weight.shape[0]
    sources = model_parts * unit_parts
    blocks = attn_out.reshape(model_parts, unit_parts, row_count, attn_out.shape[1])
    picked = lax.dynamic_index_in_dim(blocks, lax.axis_index("expert"), axis=1, keepdims=False)
    picked = picked.reshape(model_parts * row_count, attn_out.shape[1])
    projected = lax.psum_scatter(
        jnp.dot(picked, proj_weight, preferred_element_type=jnp.float32),
        "mp",
        scatter_dimension=0,
        tiled=True,
    )
    hidden_state = residual + projected
    inverse_rms = lax.rsqrt(jnp.mean(hidden_state * hidden_state, axis=1, keepdims=True) + EPSILON)
    normed = (hidden_state * inverse_rms * norm_gain).astype(jnp.bfloat16)
    expert_ids = routes.reshape(-1)
    onehot = (expert_ids[:, None] == jnp.arange(EXPERTS, dtype=jnp.int32)[None, :]).astype(
        jnp.int32
    )
    before = jnp.cumsum(onehot, axis=0) - onehot
    position = jnp.sum(before * onehot, axis=1)
    target = expert_ids * MOST + position
    placement = (jnp.arange(EXPERTS * MOST, dtype=jnp.int32)[:, None] == target[None, :]).astype(
        jnp.bfloat16
    )
    doubled = jnp.repeat(normed, 2, axis=0)
    outgoing = jnp.dot(placement, doubled, preferred_element_type=jnp.float32).astype(jnp.bfloat16)
    outgoing = outgoing.reshape(model_parts, local_experts, MOST, features)
    copies = jnp.broadcast_to(
        outgoing[:, None], (model_parts, unit_parts, local_experts, MOST, features)
    )
    copies = copies.reshape(sources, local_experts, MOST, features)
    arrived = lax.all_to_all(copies, ("mp", "expert"), split_axis=0, concat_axis=0, tiled=True)
    gate_part = jnp.einsum(
        "qemd,edf->qemf", arrived, gate_weight, preferred_element_type=jnp.float32
    )
    up_part = jnp.einsum("qemd,edf->qemf", arrived, up_weight, preferred_element_type=jnp.float32)
    activation = (jax.nn.silu(gate_part) * up_part).astype(jnp.bfloat16)
    partial_value = jnp.einsum(
        "qemf,efd->qemd", activation, down_weight, preferred_element_type=jnp.float32
    ).astype(jnp.bfloat16)
    returned = lax.all_to_all(
        partial_value, ("mp", "expert"), split_axis=0, concat_axis=0, tiled=True
    )
    returned = returned.reshape(model_parts, unit_parts, local_experts, MOST, features)
    outputs = jnp.sum(returned, axis=1, dtype=jnp.float32).astype(jnp.bfloat16)
    expert_out = outputs.reshape(EXPERTS * MOST, features)
    gathered_back = jnp.dot(placement.T, expert_out, preferred_element_type=jnp.float32)
    gathered_back = gathered_back.reshape(row_count, 2, features)
    return (
        hidden_state
        + route_weights[:, 0:1] * gathered_back[:, 0]
        + route_weights[:, 1:2] * gathered_back[:, 1]
    )


def solution(mesh):
    in_specs = (
        P("dp", "mp"),
        P(("dp", "mp", "expert"), None),
        P("mp", None),
        P(),
        P("mp", None, "expert"),
        P("mp", None, "expert"),
        P("mp", "expert", None),
        P(("dp", "mp", "expert"), None),
        P(("dp", "mp", "expert"), None),
    )
    out_specs = P(("dp", "mp", "expert"), None)
    return jax.shard_map(body, mesh=mesh, in_specs=in_specs, out_specs=out_specs, check_vma=False)
```

profile of v0, /device:TPU:0, one launch (start us, length us, event | category | flops | bytes accessed | tf_op | source)
XLA Modules:
  0.0 134.6 jit_solution(5581229104023624008)
XLA Ops:
  6.5 0.0 reduce-scatter.2.cloned.1.call-start
  6.5 1.1 copy-done
  7.6 0.0 copy-start.5
  7.6 0.0 copy-start.3
  7.6 0.0 copy-start.4
  7.7 4.2 %fusion.30 = f32[64,2304]{1,0:T(8,128)} fusion(bf16[64,1152]{1,0:T(8,128)(2,1)S(1)} %bitcast.78, bf16[1152,2304]{1,0:T(8,128)(2,1)} %param.11), kind=kOutput, calls=%fused_computation.40 | convolution fusion | flops 339738624 | bytes 6045696 | tf_op jit(solution)/shard_map/dot_general | solution.py:34
  11.9 0.0 reduce-scatter.2.cloned.1.call-update
  11.9 0.1 copy.21
  12.0 0.1 reshape.69
  12.1 0.1 fusion.27
  12.2 0.1 reduce_window_sum.11
  12.3 0.2 select_reduce_fusion
  12.5 17.6 %reduce-scatter.2.cloned.1.call-done = f32[32,2304]{1,0:T(8,128)} async-done(((f32[64,2304]{1,0:T(8,128)}), f32[32,2304]{1,0:T(8,128)}) %reduce-scatter.2.cloned.1.call-update) | async-done | bytes 294928 | tf_op jit(solution)/shard_map/reduce_scatter | solution.py:33
  30.0 1.1 multiply_reduce_fusion
  31.2 0.1 multiply_convert_fusion
  31.3 0.2 broadcast_in_dim.6
  31.4 0.1 reshape.70
  31.6 0.3 convolution_convert_fusion
  31.9 0.2 broadcast_in_dim.8
  32.1 31.9 %all_to_all.10 = bf16[8,4,16,2304]{3,2,1,0:T(8,128)(2,1)S(1)} all-to-all(bf16[8,4,16,2304]{3,2,1,0:T(8,128)(2,1)S(1)} %bitcast.75), channel_id=1, replica_groups=mesh['dp'=4,'mp'=2,'expert'=4] {'mp','expert'}, dimensions={0} | all-to-all | bytes 4718592 | tf_op jit(solution)/shard_map/all_to_all | solution.py:59
  64.0 1.4 %copy-done.2 = bf16[8,4,16,2304]{3,2,1,0:T(8,128)(2,1)} copy-done((bf16[8,4,16,2304]{3,2,1,0:T(8,128)(2,1)}, bf16[8,4,16,2304]{3,2,1,0:T(8,128)(2,1)S(1)}, u32[]{:S(2)}) %copy-start.2) | copy-done | bytes 2359320
  65.4 10.5 %fusion.2 = f32[4,8,16,1024]{3,2,1,0:T(8,128)} fusion(bf16[4,2304,1024]{2,1,0:T(8,128)(2,1)} %param.14, bf16[8,4,16,2304]{3,2,1,0:T(8,128)(2,1)S(1)} %all_to_all.10), kind=kOutput, calls=%fused_computation.2 | convolution fusion | flops 2415919104 | bytes 23330816 | tf_op jit(solution)/shard_map/qemd,edf->qemf/dot_general | solution.py:63
  76.0 11.7 %fusion.12 = bf16[8,4,16,1024]{3,2,0,1:T(8,128)(2,1)} fusion(f32[4,8,16,1024]{3,2,1,0:T(8,128)} %fusion.2, bf16[4,2304,1024]{2,1,0:T(8,128)(2,1)} %param.13, bf16[8,4,16,2304]{3,2,1,0:T(8,128)(2,1)} %copy-done.2), kind=kOutput, calls=%fused_computation.11 | convolution fusion | flops 2419064832 | bytes 24379392 | tf_op jit(solution)/shard_map/qemd,edf->qemf/dot_general | solution.py:60
  87.7 3.9 %fusion.9 = bf16[8,4,16,2304]{3,2,0,1:T(8,128)(2,1)S(1)} fusion(bf16[8,4,16,1024]{3,2,0,1:T(8,128)(2,1)} %fusion.12, bf16[4,1024,2304]{2,1,0:T(8,128)(2,1)S(1)} %bitcast.74), kind=kOutput, calls=%fused_computation.7 | convolution fusion | flops 2417098752 | bytes 22282240 | tf_op jit(solution)/shard_map/qemf,efd->qemd/dot_general | solution.py:65
  91.6 1.6 %copy.24 = bf16[8,4,16,2304]{3,2,1,0:T(8,128)(2,1)} copy(bf16[8,4,16,2304]{3,2,0,1:T(8,128)(2,1)S(1)} %fusion.9) | data formatting | bytes 4718592 | tf_op jit(solution)/shard_map/convert_element_type | solution.py:67
  93.2 3.7 %all-to-all-start.1 = ((bf16[8,4,16,2304]{3,2,1,0:T(8,128)(2,1)}), bf16[8,4,16,2304]{3,2,1,0:T(8,128)(2,1)S(1)}, u32[]{:S(2)}, u32[]{:S(2)}) async-start(bf16[8,4,16,2304]{3,2,1,0:T(8,128)(2,1)} %copy.24), calls=%async_computation.2 | async-start | bytes 4718592 | tf_op jit(solution)/shard_map/all_to_all | solution.py:68
  97.0 0.1 iota_compare_fusion.3
  97.1 0.0 copy-start.1
  97.1 29.2 %all-to-all-done.1 = bf16[8,4,16,2304]{3,2,1,0:T(8,128)(2,1)S(1)} async-done(((bf16[8,4,16,2304]{3,2,1,0:T(8,128)(2,1)}), bf16[8,4,16,2304]{3,2,1,0:T(8,128)(2,1)S(1)}, u32[]{:S(2)}, u32[]{:S(2)}) %all-to-all-start.1) | async-done | bytes 2359328 | tf_op jit(solution)/shard_map/all_to_all | solution.py:68
  126.4 0.3 bitcast_reduce_fusion
  126.7 0.2 fusion.28
  127.0 0.8 fusion.23
  (24 shorter events, 0.1 us)
Async XLA Ops:
  6.5 1.1 copy-start
  6.5 23.5 %reduce-scatter.2.cloned.1.call-start = ((), (), s32[]{:S(2)}) async-start(), calls=%async_computation.3 | async-start | bytes 884736 | tf_op jit(solution)/shard_map/reduce_scatter | solution.py:33
  7.6 4.3 %copy-start.5 = (s32[32,2]{0,1:T(2,128)S(1)}, s32[32,2]{0,1:T(2,128)}, u32[]{:S(2)}) copy-start(s32[32,2]{0,1:T(2,128)} %param.16) | copy-start | bytes 772
  7.6 22.4 %copy-start.3 = (f32[32,2304]{1,0:T(8,128)S(1)}, f32[32,2304]{1,0:T(8,128)}, u32[]{:S(2)}) copy-start(f32[32,2304]{1,0:T(8,128)} %param.10) | copy-start | bytes 884740
  7.6 23.5 %copy-start.4 = (f32[2304]{0:T(1024)S(1)}, f32[2304]{0:T(1024)}, u32[]{:S(2)}) copy-start(f32[2304]{0:T(1024)} %param.12) | copy-start | bytes 27652
  64.0 1.4 %copy-start.2 = (bf16[8,4,16,2304]{3,2,1,0:T(8,128)(2,1)}, bf16[8,4,16,2304]{3,2,1,0:T(8,128)(2,1)S(1)}, u32[]{:S(2)}) copy-start(bf16[8,4,16,2304]{3,2,1,0:T(8,128)(2,1)S(1)} %all_to_all.10) | copy-start | bytes 7077892
  65.4 22.3 %slice-start = ((s8[18874368]{0:T(1024)(128)(4,1)}), s8[4194304]{0:T(1024)(128)(4,1)S(1)}, s32[]{:S(2)}) async-start(s8[18874368]{0:T(1024)(128)(4,1)} %bitcast.73), calls=%async_computation.4 | async-start | bytes 8388608
  65.4 22.3 %slice-start.1 = ((s8[18874368]{0:T(1024)(128)(4,1)}), s8[4194304]{0:T(1024)(128)(4,1)S(1)}, s32[]{:S(2)}) async-start(s8[18874368]{0:T(1024)(128)(4,1)} %bitcast.73), calls=%async_computation.5 | async-start | bytes 8388608
  65.4 22.3 %slice-start.2 = ((s8[18874368]{0:T(1024)(128)(4,1)}), s8[4194304]{0:T(1024)(128)(4,1)S(1)}, s32[]{:S(2)}) async-start(s8[18874368]{0:T(1024)(128)(4,1)} %bitcast.73), calls=%async_computation.6 | async-start | bytes 8388608
  75.9 11.7 %slice-start.3 = ((s8[18874368]{0:T(1024)(128)(4,1)}), s8[4194304]{0:T(1024)(128)(4,1)S(1)}, s32[]{:S(2)}) async-start(s8[18874368]{0:T(1024)(128)(4,1)} %bitcast.73), calls=%async_computation.7 | async-start | bytes 8388608
  76.0 11.7 %slice-start.4 = ((s8[18874368]{0:T(1024)(128)(4,1)}), s8[2097152]{0:T(1024)(128)(4,1)S(1)}, s32[]{:S(2)}) async-start(s8[18874368]{0:T(1024)(128)(4,1)} %bitcast.73), calls=%async_computation.8 | async-start | bytes 4194304
  93.2 3.9 %copy-start.6 = (f32[32,2]{0,1:T(2,128)S(1)}, f32[32,2]{0,1:T(2,128)}, u32[]{:S(2)}) copy-start(f32[32,2]{0,1:T(2,128)} %param.17) | copy-start | bytes 772
  93.2 33.1 %all-to-all-start.1 = ((bf16[8,4,16,2304]{3,2,1,0:T(8,128)(2,1)}), bf16[8,4,16,2304]{3,2,1,0:T(8,128)(2,1)S(1)}, u32[]{:S(2)}, u32[]{:S(2)}) async-start(bf16[8,4,16,2304]{3,2,1,0:T(8,128)(2,1)} %copy.24), calls=%async_computation.2 | async-start | bytes 4718592 | tf_op jit(solution)/shard_map/all_to_all | solution.py:68
  97.1 30.7 %copy-start.1 = (bf16[256,1152]{1,0:T(8,128)(2,1)S(1)}, bf16[256,1152]{1,0:T(8,128)(2,1)}, u32[]{:S(2)}) copy-start(bf16[256,1152]{1,0:T(8,128)(2,1)} %param.9) | copy-start | bytes 1769476
Sparse Core Ops, SparseCore 0:
  12.0 17.9 reduce-scatter.1
where the time goes:
time: 135 us
  waiting for transfers between devices  46.8 us (35%)
  blocking collectives  31.9 us (24%)
  matrix products  30.9 us (23%)
  between operations  13.6 us (10%)
  local copies, waits for them, and re-layouts  4.8 us (4%)
  starting transfers between devices  3.75 us (3%)
  other arithmetic  2.8 us (2%)
    all_to_all x1, blocking collectives, body(): lax.all_to_all(copies, ('mp', 'expert'), split_axis=0, concat_axis=0, til...  31.9 us
    all_to_all x1, waiting for transfers between devices, body(): lax.all_to_all(partial_value, ('mp', 'expert'), split_axis=0, concat_axis...  29.2 us
    reduce_scatter x1, waiting for transfers between devices, body(): lax.psum_scatter(jnp.dot(picked, proj_weight, preferred_element_type=jnp....  17.6 us
    dot_general x1, matrix products, body(): jnp.einsum('qemd,edf->qemf', arrived, gate_weight, preferred_element_type...  11.7 us
    dot_general x1, matrix products, body(): jnp.einsum('qemd,edf->qemf', arrived, up_weight, preferred_element_type=j...  10.5 us
    dot_general x1, matrix products, body(): jnp.dot(picked, proj_weight, preferred_element_type=jnp.float32)  4.23 us
    dot_general x1, matrix products, body(): jnp.einsum('qemf,efd->qemd', activation, down_weight, preferred_element_t...  3.93 us
    all_to_all x1, starting transfers between devices, body(): lax.all_to_all(partial_value, ('mp', 'expert'), split_axis=0, concat_axis...  3.75 us
  transfers between devices with their start and end apart: 2, of which 2 were waited for; matrix products, arithmetic and copies ran while one was open for 0% of the time, Pallas kernels for 0%

commit v1 on v0

v1 whole, which is shorter than its diff:
```python
import functools

import jax
import jax.numpy as jnp
from jax import lax
from jax.experimental import pallas as pl
from jax.experimental.pallas import tpu as pltpu
from jax.sharding import PartitionSpec as P

MOST = 16
EPSILON = 1e-06
LANES = 128
TILE = 256
WIDE = 768
SLOTS = 3
MESH = pl.DeviceIdType.MESH
BF16 = jnp.bfloat16
F32 = jnp.float32


def dot(a, b):
    return jnp.dot(a, b, preferred_element_type=F32)


def kernel(
    sizes,
    attn_ref,
    residual_ref,
    proj_ref,
    gain_ref,
    gate_ref,
    up_ref,
    down_ref,
    meta_ref,
    out_ref,
    picked,
    gates,
    ups,
    downs,
    shared,
    psend,
    precv,
    hidden,
    gathered,
    metas,
    place,
    comb,
    scale,
    rows,
    act,
    block,
    part,
    sib,
    ssend,
    rrecv,
    pick_sem,
    proj_sem,
    gate_sem,
    up_sem,
    down_sem,
    meta_send,
    meta_recv,
    part_send,
    part_recv,
    row_send,
    row_recv,
    fwd_send,
    fwd_recv,
    sib_send,
    sib_recv,
    ret_send,
    ret_recv,
):
    mp, ex, rc, nl, depth, chunks = sizes
    group, half, pairs = mp * ex, mp * ex // 2, ex // 2
    units = gate_ref.shape[2]
    feats = residual_ref.shape[1]
    total = group * rc
    slots = group * MOST
    m, e = lax.axis_index("mp"), lax.axis_index("expert")
    g = m * ex + e
    c = lax.rem(e, 2)
    h = lax.div(g, 2)
    sibling = {"expert": e + 1 - 2 * c}

    def peer(index):
        return {"mp": lax.div(index, ex), "expert": lax.rem(index, ex)}

    picks = []
    for d in range(mp):
        owner = lax.rem(m + d, mp) * ex + e
        picks.append(
            pltpu.make_async_copy(
                attn_ref.at[pl.ds(pl.multiple_of(owner * rc, rc), rc), :],
                picked.at[pl.ds(d * rc, rc), :],
                pick_sem.at[d],
            )
        )
    projs = [
        pltpu.make_async_copy(
            proj_ref.at[:, pl.ds(j * WIDE, WIDE)],
            shared.at[pl.ds(0, depth), pl.ds(j * WIDE, WIDE)],
            proj_sem.at[j],
        )
        for j in range(chunks)
    ]
    gate_in = [
        pltpu.make_async_copy(gate_ref.at[l], gates.at[l % SLOTS], gate_sem.at[l])
        for l in range(nl)
    ]
    up_in = [
        pltpu.make_async_copy(up_ref.at[l], ups.at[l % SLOTS], up_sem.at[l]) for l in range(nl)
    ]

    def down_at(l):
        return shared.at[pl.ds(0, units), :] if l == nl - 1 else downs.at[l]

    down_in = [
        pltpu.make_async_copy(down_ref.at[l], down_at(l), down_sem.at[l]) for l in range(nl)
    ]
    for copy in picks + projs:
        copy.start()

    barrier = pltpu.get_barrier_semaphore()
    for d in range(1, group):
        pl.semaphore_signal(
            barrier, inc=1, device_id=peer(lax.rem(g + d, group)), device_id_type=MESH
        )
    pl.semaphore_wait(barrier, group - 1)

    metas[g] = meta_ref[...]
    meta_out = [
        pltpu.make_async_remote_copy(
            src_ref=meta_ref,
            dst_ref=metas.at[g],
            send_sem=meta_send.at[d - 1],
            recv_sem=meta_recv.at[d - 1],
            device_id=peer(lax.rem(g + d, group)),
            device_id_type=MESH,
        )
        for d in range(1, group)
    ]
    for copy in meta_out:
        copy.start()
    for copy in picks:
        copy.wait()

    part_out = []
    for j in range(chunks):
        projs[j].wait()
        if j == 0:
            for l in range(min(SLOTS, nl)):
                gate_in[l].start()
                up_in[l].start()
            for l in range(nl - 1):
                down_in[l].start()
        cols = pl.ds(j * WIDE, WIDE)
        value = dot(picked[...], shared[pl.ds(0, depth), cols])
        hidden[:, cols] = residual_ref[:, cols] + value[0:rc]
        for d in range(1, mp):
            psend[j, d - 1] = value[d * rc : (d + 1) * rc].astype(BF16)
            copy = pltpu.make_async_remote_copy(
                src_ref=psend.at[j, d - 1],
                dst_ref=precv.at[j, d - 1],
                send_sem=part_send.at[j, d - 1],
                recv_sem=part_recv.at[j, d - 1],
                device_id={"mp": lax.rem(m + d, mp)},
                device_id_type=MESH,
            )
            copy.start()
            part_out.append((j, d, copy))
    down_in[nl - 1].start()

    for copy in meta_out:
        copy.wait_recv()
    per = LANES // rc
    lanes = []
    for q in range(group // per):
        merged = metas[q * per]
        for i in range(1, per):
            merged = merged + metas[q * per + i]
        lanes.append(merged)
    table = jnp.concatenate(lanes, axis=1)
    first, second = table[0:1], table[1:2]
    ids = (lax.broadcasted_iota(jnp.int32, (16, total), 0) + m * nl).astype(F32)
    is_first = first == ids
    named = jnp.where(is_first, 1.0, jnp.where(second == ids, 1.0, 0.0))
    weight = jnp.where(is_first, table[2:3], table[3:4])
    row_at = lax.broadcasted_iota(jnp.int32, (total, total), 0)
    col_at = lax.broadcasted_iota(jnp.int32, (total, total), 1)
    earlier = jnp.where((row_at // rc == col_at // rc) & (row_at < col_at), 1.0, 0.0)
    rank = dot(named.astype(BF16), earlier.astype(BF16))
    base = (lax.broadcasted_iota(jnp.int32, (16, total), 1) // rc * MOST).astype(F32)
    target = jnp.where(named > 0.5, rank + base, -1.0)
    slot_at = lax.broadcasted_iota(jnp.int32, (slots, total), 0).astype(F32)
    for l in range(nl):
        hit = jnp.where(slot_at == target[l : l + 1], 1.0, 0.0)
        here = pl.ds(l * slots, slots)
        place[here, :] = hit.astype(BF16)
        comb[:, here] = hit.T.astype(BF16)
        scale[here, :] = jnp.sum(hit * weight[l : l + 1], axis=1, keepdims=True)

    for j, d, copy in part_out:
        copy.wait_recv()
        cols = pl.ds(j * WIDE, WIDE)
        hidden[:, cols] = hidden[:, cols] + precv[j, d - 1].astype(F32)
    state = hidden[...]
    inverse = lax.rsqrt(jnp.mean(state * state, axis=1, keepdims=True) + EPSILON)
    gathered[g] = (state * inverse * gain_ref[...]).astype(BF16)

    row_out = []
    for d in range(1, half):
        row_out.append(
            pltpu.make_async_remote_copy(
                src_ref=gathered.at[g],
                dst_ref=gathered.at[g],
                send_sem=row_send.at[d - 1],
                recv_sem=row_recv.at[d - 1],
                device_id=peer(2 * lax.rem(h + d, half) + c),
                device_id_type=MESH,
            )
        )
        row_out[-1].start()
    fwd_out = []
    for d in range(half):
        if d > 0:
            row_out[d - 1].wait_recv()
        source = 2 * lax.rem(h + half - d, half) + c
        fwd_out.append(
            pltpu.make_async_remote_copy(
                src_ref=gathered.at[source],
                dst_ref=gathered.at[source],
                send_sem=fwd_send.at[d],
                recv_sem=fwd_recv.at[d],
                device_id=sibling,
                device_id_type=MESH,
            )
        )
        fwd_out[-1].start()
    for copy in fwd_out:
        copy.wait_recv()

    @pl.loop(0, feats // TILE)
    def _(t):
        cols = pl.ds(pl.multiple_of(t * TILE, TILE), TILE)
        source = gathered[:, :, cols].reshape(total, TILE)
        rows[:, cols] = dot(place[...], source).astype(BF16)

    for l in range(nl):
        gate_in[l].wait()
        up_in[l].wait()
        here = pl.ds(l * slots, slots)

        @pl.loop(0, units // TILE)
        def _(t):
            cols = pl.ds(pl.multiple_of(t * TILE, TILE), TILE)
            gate = dot(rows[here, :], gates[l % SLOTS, :, cols])
            up = dot(rows[here, :], ups[l % SLOTS, :, cols])
            act[here, cols] = (gate / (1.0 + jnp.exp(-gate)) * up).astype(BF16)

        if l + SLOTS < nl:
            gate_in[l + SLOTS].start()
            up_in[l + SLOTS].start()

    for copy in down_in:
        copy.wait()

    sib_out, ret_out = [], []

    def pass_on(j):
        sib_out[j].wait_recv()
        ssend[j] = (part[j, c].astype(F32) + sib[j].astype(F32)).astype(BF16)
        for d in range(1, half):
            copy = pltpu.make_async_remote_copy(
                src_ref=ssend.at[j, lax.rem(h + d, half)],
                dst_ref=rrecv.at[j, d - 1],
                send_sem=ret_send.at[j, d - 1],
                recv_sem=ret_recv.at[j, d - 1],
                device_id=peer(2 * lax.rem(h + d, half) + c),
                device_id_type=MESH,
            )
            copy.start()
            ret_out.append((j, d, copy))

    for j in range(chunks):

        @pl.loop(0, WIDE // TILE)
        def _(t):
            to = pl.ds(pl.multiple_of(t * TILE, TILE), TILE)
            cols = pl.ds(pl.multiple_of(j * WIDE + t * TILE, TILE), TILE)
            for l in range(nl):
                here = pl.ds(l * slots, slots)
                matrix = shared[pl.ds(0, units), cols] if l == nl - 1 else downs[l, :, cols]
                block[here, :] = (dot(act[here, :], matrix) * scale[here, :]).astype(BF16)
            mixed = dot(comb[...], block[...]).astype(BF16)
            for index in range(group):
                part[j, index % 2, index // 2, :, to] = mixed[index * rc : (index + 1) * rc]

        copy = pltpu.make_async_remote_copy(
            src_ref=part.at[j, 1 - c],
            dst_ref=sib.at[j],
            send_sem=sib_send.at[j],
            recv_sem=sib_recv.at[j],
            device_id=sibling,
            device_id_type=MESH,
        )
        copy.start()
        sib_out.append(copy)
        if j > 0:
            pass_on(j - 1)
    pass_on(chunks - 1)

    for j in range(chunks):
        cols = pl.ds(j * WIDE, WIDE)
        value = ssend[j, h].astype(F32)
        for at, d, copy in ret_out:
            if at == j:
                copy.wait_recv()
                value = value + rrecv[j, d - 1].astype(F32)
        out_ref[:, cols] = hidden[:, cols] + value

    for copy in meta_out + row_out + fwd_out + sib_out:
        copy.wait_send()
    for _, _, copy in part_out + ret_out:
        copy.wait_send()


def body(
    attn_out,
    residual,
    proj_weight,
    norm_gain,
    gate_weight,
    up_weight,
    down_weight,
    routes,
    route_weights,
):
    mp = lax.axis_size("mp")
    ex = lax.axis_size("expert")
    rc, feats = residual.shape
    nl, _, units = gate_weight.shape
    depth = proj_weight.shape[0]
    group, half = mp * ex, mp * ex // 2
    total, slots = group * rc, nl * group * MOST
    chunks = feats // WIDE
    per = LANES // rc
    index = lax.axis_index("mp") * ex + lax.axis_index("expert")
    pairs = jnp.concatenate([routes.astype(F32), route_weights], axis=1).T
    meta = lax.dynamic_update_slice(
        jnp.zeros((8, LANES), F32), pairs, (jnp.int32(0), lax.rem(index, per) * rc)
    )
    vmem = pl.BlockSpec(memory_space=pltpu.VMEM)
    hbm = pl.BlockSpec(memory_space=pl.ANY)
    dma = pltpu.SemaphoreType.DMA
    return pl.pallas_call(
        functools.partial(kernel, (mp, ex, rc, nl, depth, chunks)),
        out_shape=jax.ShapeDtypeStruct((rc, feats), F32),
        in_specs=[hbm, vmem, hbm, vmem, hbm, hbm, hbm, vmem],
        out_specs=vmem,
        scratch_shapes=[
            pltpu.VMEM((mp * rc, depth), BF16),
            pltpu.VMEM((min(SLOTS, nl), feats, units), BF16),
            pltpu.VMEM((min(SLOTS, nl), feats, units), BF16),
            pltpu.VMEM((max(nl - 1, 1), units if nl > 1 else 16, feats), BF16),
            pltpu.VMEM((max(depth, units), feats), BF16),
            pltpu.VMEM((chunks, mp - 1, rc, WIDE), BF16),
            pltpu.VMEM((chunks, mp - 1, rc, WIDE), BF16),
            pltpu.VMEM((rc, feats), F32),
            pltpu.VMEM((group, rc, feats), BF16),
            pltpu.VMEM((group, 8, LANES), F32),
            pltpu.VMEM((slots, total), BF16),
            pltpu.VMEM((total, slots), BF16),
            pltpu.VMEM((slots, 1), F32),
            pltpu.VMEM((slots, feats), BF16),
            pltpu.VMEM((slots, units), BF16),
            pltpu.VMEM((slots, TILE), BF16),
            pltpu.VMEM((chunks, 2, half, rc, WIDE), BF16),
            pltpu.VMEM((chunks, half, rc, WIDE), BF16),
            pltpu.VMEM((chunks, half, rc, WIDE), BF16),
            pltpu.VMEM((chunks, half - 1, rc, WIDE), BF16),
            dma((mp,)),
            dma((chunks,)),
            dma((nl,)),
            dma((nl,)),
            dma((nl,)),
            dma((group - 1,)),
            dma((group - 1,)),
            dma((chunks, mp - 1)),
            dma((chunks, mp - 1)),
            dma((half - 1,)),
            dma((half - 1,)),
            dma((half,)),
            dma((half,)),
            dma((chunks,)),
            dma((chunks,)),
            dma((chunks, half - 1)),
            dma((chunks, half - 1)),
        ],
        compiler_params=pltpu.CompilerParams(
            collective_id=0, has_side_effects=True, vmem_limit_bytes=62 * 1024 * 1024
        ),
    )(
        attn_out,
        residual,
        proj_weight,
        norm_gain.reshape(1, feats),
        gate_weight,
        up_weight,
        down_weight,
        meta,
    )


def solution(mesh):
    in_specs = (
        P("dp", "mp"),
        P(("dp", "mp", "expert"), None),
        P("mp", None),
        P(),
        P("mp", None, "expert"),
        P("mp", None, "expert"),
        P("mp", "expert", None),
        P(("dp", "mp", "expert"), None),
        P(("dp", "mp", "expert"), None),
    )
    out_specs = P(("dp", "mp", "expert"), None)
    return jax.shard_map(body, mesh=mesh, in_specs=in_specs, out_specs=out_specs, check_vma=False)
```

time: 135 us -> 49.9 us (0.37)
  waiting for transfers between devices: 46.8 us -> 0 us
  Pallas kernels: 0 us -> 44.9 us
  blocking collectives: 31.9 us -> 0 us
  matrix products: 30.9 us -> 0 us
  between operations: 13.6 us -> 0.03 us
  starting transfers between devices: 3.75 us -> 0 us
  local copies, waits for them, and re-layouts: 4.8 us -> 3.33 us
  other arithmetic: 2.8 us -> 1.37 us
    pallas_call x0 -> x1, Pallas kernels: none -> 44.9 us  [body(): pl.pallas_call(functools.partial(kernel, (mp, ex, rc, nl, depth, chunks))...]
    all_to_all x1 -> x0, blocking collectives: 31.9 us -> none  [body(): lax.all_to_all(copies, ('mp', 'expert'), split_axis=0, concat_axis=0, til...]
    dot_general x6 -> x0, matrix products: 30.9 us -> none  [the longest x1 11.7 us: body(): jnp.einsum('qemd,edf->qemf', arrived, gate_weight, preferred_element_type...]
    all_to_all x1 -> x0, waiting for transfers between devices: 29.2 us -> none  [body(): lax.all_to_all(partial_value, ('mp', 'expert'), split_axis=0, concat_axis...]
    reduce_scatter x1 -> x0, waiting for transfers between devices: 17.6 us -> none  [body(): lax.psum_scatter(jnp.dot(picked, proj_weight, preferred_element_type=jnp....]
    all_to_all x1 -> x0, starting transfers between devices: 3.75 us -> none  [body(): lax.all_to_all(partial_value, ('mp', 'expert'), split_axis=0, concat_axis...]
    reduce_sum x3 -> x0, other arithmetic: 1.61 us -> none  [the longest x1 1.1 us: body(): jnp.mean(hidden_state * hidden_state, axis=1, keepdims=True) + EPSILON]
    convert_element_type x1 -> x0, local copies, waits for them, and re-layouts: 1.6 us -> none  [body(): partial_value = jnp.einsum('qemf,efd->qemd', activation, down_weight, pre...]
  transfers between devices with their start and end apart: 2 -> 0, of which waited for: 2 -> 0; matrix products, arithmetic and copies ran while one was open for 0% -> 0% of each run, Pallas kernels for 0% -> 0%
where the time goes in v1:
time: 49.9 us; the launch traced here: 49.6 us
  Pallas kernels  44.9 us (90%)
  local copies, waits for them, and re-layouts  3.33 us (7%)
  other arithmetic  1.37 us (3%)
    pallas_call x1, Pallas kernels, body(): pl.pallas_call(functools.partial(kernel, (mp, ex, rc, nl, depth, chunks))...  44.9 us
    unnamed x3, local copies, waits for them, and re-layouts  1.7 us
    reshape x1, local copies, waits for them, and re-layouts, body(): norm_gain.reshape(1, feats)  1.31 us

profile of v1, /device:TPU:0, one launch (start us, length us, event | category | flops | bytes accessed | tf_op | source)
XLA Modules:
  0.0 49.6 jit_solution(4976080203399468376)
XLA Ops:
  0.0 0.7 %convert_element_type.3 = f32[32,2]{0,1:T(2,128)S(1)} convert(s32[32,2]{0,1:T(2,128)} %param.16) | non-fusion elementwise | flops 64 | bytes 512 | tf_op jit(solution)/shard_map/convert_element_type | solution.py:349
  0.7 0.7 %maximum_bitcast_fusion = f32[4,32]{1,0:T(4,128)S(1)} fusion(f32[32,2]{0,1:T(2,128)} %param.17, f32[32,2]{0,1:T(2,128)S(1)} %convert_element_type.3), kind=kLoop, calls=%fused_computation | loop fusion | flops 128 | bytes 1024 | tf_op jit(solution)/shard_map/transpose | solution.py:349
  1.4 0.3 dynamic_update_slice.3.meta_ref
  1.7 0.0 copy-start
  1.7 1.3 %reshape.3.gain_ref = f32[1,2304]{1,0:T(1,128)} reshape(f32[2304]{0:T(1024)} %param.12) | data formatting | bytes 18432 | tf_op jit(solution)/shard_map/reshape | solution.py:407
  3.0 0.0 copy-done
  3.0 44.9 %shard_map.91 = f32[32,2304]{1,0:T(8,128)} custom-call(bf16[256,1152]{1,0:T(8,128)(2,1)} %attn_ref.1, f32[32,2304]{1,0:T(8,128)} %residual_ref.1, bf16[1152,2304]{1,0:T(8,128)(2,1)} %proj_ref.1, f32[1,2304]{1,0:T(1,128)} %reshape.3.gain_ref, bf16[4,2304,1024]{2,1,0:T(8,128)(2,1)} %gate_ref.1, bf16[4,2304,1024]{2,1,0:T(8,128)(2,1)} %up_ref.1, ...), custom_call_target="tpu_custom_call" | custom-call | tf_op jit(solution)/shard_map/pallas_call | solution.py:356
  47.9 1.7 %copy.12 = f32[32,2304]{1,0:T(8,128)} copy(f32[32,2304]{1,0:T(8,128)} %shard_map.91) | data formatting | bytes 589824
  (1 shorter events, 0.0 us)
Async XLA Ops:
  1.7 1.3 %copy-start = (f32[8,128]{1,0:T(8,128)}, f32[8,128]{1,0:T(8,128)S(1)}, u32[]{:S(2)}) copy-start(f32[8,128]{1,0:T(8,128)S(1)} %dynamic_update_slice.3.meta_ref) | copy-start | bytes 12292

commit v2 on v1

v2 whole, which is shorter than its diff:
```python
import functools

import jax
import jax.numpy as jnp
from jax import lax
from jax.experimental import pallas as pl
from jax.experimental.pallas import tpu as pltpu
from jax.sharding import PartitionSpec as P

MOST = 16
EPSILON = 1e-06
LANES = 128
TILE = 256
WIDE = 768
MESH = pl.DeviceIdType.MESH
BF16 = jnp.bfloat16
F32 = jnp.float32


def dot(a, b):
    return jnp.dot(a, b, preferred_element_type=F32)


def kernel(
    sizes,
    attn_ref,
    residual_ref,
    proj_ref,
    gain_ref,
    gate_ref,
    up_ref,
    down_ref,
    routes_ref,
    weights_ref,
    out_ref,
    picked,
    res,
    gate_big,
    up_big,
    gate_small,
    up_small,
    down_small,
    proj,
    psend,
    precv,
    psum,
    gathered0,
    gathered1,
    gathered2,
    metas,
    place,
    comb,
    rows,
    gate_acc,
    up_acc,
    act,
    block,
    part32,
    part,
    sib,
    ssend,
    rrecv,
    pick_sem,
    res_sem,
    proj_sem,
    gate_sem,
    up_sem,
    down_sem,
    meta_send,
    meta_recv,
    part_send,
    part_recv,
    row_send,
    row_recv,
    fwd_send,
    fwd_recv,
    sib_send,
    sib_recv,
    ret_send,
    ret_recv,
):
    mp, ex, rc, nl = sizes
    group, half = mp * ex, mp * ex // 2
    units = gate_ref.shape[2]
    feats = residual_ref.shape[1]
    rest = feats - 2 * units
    spans = [(0, units), (units, units), (2 * units, rest)]
    gathered = [gathered0, gathered1, gathered2]
    total = group * rc
    slots = group * MOST
    m, e = lax.axis_index("mp"), lax.axis_index("expert")
    g = m * ex + e
    c = lax.rem(e, 2)
    h = lax.div(g, 2)
    sibling = {"expert": e + 1 - 2 * c}

    def peer(index):
        return {"mp": lax.div(index, ex), "expert": lax.rem(index, ex)}

    def remote(src, dst, send, recv, to):
        return pltpu.make_async_remote_copy(
            src_ref=src, dst_ref=dst, send_sem=send, recv_sem=recv, device_id=to, device_id_type=MESH
        )

    picks = []
    for d in range(mp):
        owner = lax.rem(m + d, mp) * ex + e
        picks.append(
            pltpu.make_async_copy(
                attn_ref.at[pl.ds(pl.multiple_of(owner * rc, rc), rc), :],
                picked.at[pl.ds(d * rc, rc), :],
                pick_sem.at[d],
            )
        )
    projs = [
        pltpu.make_async_copy(
            proj_ref.at[:, pl.ds(j * WIDE, WIDE)], proj.at[:, pl.ds(j * WIDE, WIDE)], proj_sem.at[j]
        )
        for j in range(feats // WIDE)
    ]
    res_in = pltpu.make_async_copy(residual_ref, res, res_sem)

    def gate_at(l, k):
        return gate_small.at[l] if k == 2 else gate_big.at[l, k]

    def up_at(l, k):
        return up_small.at[l] if k == 2 else up_big.at[l, k]

    def down_at(l, k):
        return (gate_big.at[l, 0], up_big.at[l, 0], down_small.at[l])[k]

    def load(ref, to, sem, l, k):
        start, size = spans[k]
        return pltpu.make_async_copy(ref.at[l, pl.ds(start, size), :], to(l, k), sem.at[l, k])

    experts = range(nl)
    gate_in = [[load(gate_ref, gate_at, gate_sem, l, k) for k in range(3)] for l in experts]
    up_in = [[load(up_ref, up_at, up_sem, l, k) for k in range(3)] for l in experts]
    down_in = [
        [
            pltpu.make_async_copy(
                down_ref.at[l, :, pl.ds(spans[k][0], spans[k][1])],
                down_at(l, k),
                down_sem.at[l, k],
            )
            for k in range(3)
        ]
        for l in experts
    ]
    for copy in picks + projs + [res_in]:
        copy.start()

    barrier = pltpu.get_barrier_semaphore()
    for d in range(1, group):
        pl.semaphore_signal(
            barrier, inc=1, device_id=peer(lax.rem(g + d, group)), device_id_type=MESH
        )

    per = LANES // rc
    lane = lax.broadcasted_iota(jnp.int32, (2, LANES), 1)
    mine = lane // rc == lax.rem(g, per)
    lines = [
        jnp.where(mine, jnp.concatenate([value] * per, axis=1), 0.0)
        for value in (routes_ref[...].astype(F32), weights_ref[...])
    ]
    metas[g] = jnp.concatenate(lines + [jnp.zeros((4, LANES), F32)], axis=0)
    pl.semaphore_wait(barrier, group - 1)

    meta_out = [
        remote(
            metas.at[g],
            metas.at[g],
            meta_send.at[d - 1],
            meta_recv.at[d - 1],
            peer(lax.rem(g + d, group)),
        )
        for d in range(1, group)
    ]
    for copy in meta_out:
        copy.start()
    for copy in picks:
        copy.wait()

    part_out = []
    for j in range(feats // WIDE):
        projs[j].wait()
        if j == 0:
            for k in range(3):
                for l in experts:
                    gate_in[l][k].start()
                    up_in[l][k].start()
            for l in experts:
                down_in[l][2].start()
        cols = pl.ds(j * WIDE, WIDE)
        value = dot(picked[...], proj[:, cols])
        psum[:, cols] = value[0:rc]
        for d in range(1, mp):
            psend[j, d - 1] = value[d * rc : (d + 1) * rc].astype(BF16)
            copy = remote(
                psend.at[j, d - 1],
                precv.at[j, d - 1],
                part_send.at[j, d - 1],
                part_recv.at[j, d - 1],
                {"mp": lax.rem(m + d, mp)},
            )
            copy.start()
            part_out.append((j, d, copy))

    for copy in meta_out:
        copy.wait_recv()
    lanes = []
    for q in range(group // per):
        merged = metas[q * per]
        for i in range(1, per):
            merged = merged + metas[q * per + i]
        lanes.append(merged)
    table = jnp.concatenate(lanes, axis=1)
    first, second = table[0:1], table[1:2]
    ids = (lax.broadcasted_iota(jnp.int32, (16, total), 0) + m * nl).astype(F32)
    is_first = first == ids
    named = jnp.where(is_first, 1.0, jnp.where(second == ids, 1.0, 0.0))
    weight = jnp.where(is_first, table[2:3], table[3:4])
    row_at = lax.broadcasted_iota(jnp.int32, (total, total), 0)
    col_at = lax.broadcasted_iota(jnp.int32, (total, total), 1)
    earlier = jnp.where((row_at // rc == col_at // rc) & (row_at < col_at), 1.0, 0.0)
    rank = dot(named.astype(BF16), earlier.astype(BF16))
    base = (lax.broadcasted_iota(jnp.int32, (16, total), 1) // rc * MOST).astype(F32)
    target = jnp.where(named > 0.5, rank + base, -1.0)
    slot_at = lax.broadcasted_iota(jnp.int32, (slots, total), 0).astype(F32)
    for l in experts:
        hit = slot_at == target[l : l + 1]
        here = pl.ds(l * slots, slots)
        place[here, :] = jnp.where(hit, 1.0, 0.0).astype(BF16)
        share = jnp.where(hit, weight[l : l + 1], 0.0).T
        high = share.astype(BF16)
        comb[pl.ds(0, total), here] = high
        comb[pl.ds(total, total), here] = (share - high.astype(F32)).astype(BF16)

    res_in.wait()
    for j, d, copy in part_out:
        copy.wait_recv()
        cols = pl.ds(j * WIDE, WIDE)
        psum[:, cols] = psum[:, cols] + precv[j, d - 1].astype(F32)
    state = res[...] + psum[...]
    inverse = lax.rsqrt(jnp.mean(state * state, axis=1, keepdims=True) + EPSILON)
    normed = (state * inverse * gain_ref[...].reshape(1, feats)).astype(BF16)

    row_out, fwd_out = [], []
    for k, (start, size) in enumerate(spans):
        gathered[k][g] = normed[:, start : start + size]
        row_out.append([])
        for d in range(1, half):
            row_out[k].append(
                remote(
                    gathered[k].at[g],
                    gathered[k].at[g],
                    row_send.at[k, d - 1],
                    row_recv.at[k, d - 1],
                    peer(2 * lax.rem(h + d, half) + c),
                )
            )
            row_out[k][-1].start()
        fwd_out.append([])
        for d in range(half):
            source = 2 * lax.rem(h + half - d, half) + c
            fwd_out[k].append(
                remote(
                    gathered[k].at[source],
                    gathered[k].at[source],
                    fwd_send.at[k, d],
                    fwd_recv.at[k, d],
                    sibling,
                )
            )
        fwd_out[k][0].start()

    def forward(k):
        for d in range(1, half):
            row_out[k][d - 1].wait_recv()
            fwd_out[k][d].start()

    forward(0)
    for k, (start, size) in enumerate(spans):
        for copy in fwd_out[k]:
            copy.wait_recv()

        @pl.loop(0, size // TILE)
        def _(t):
            cols = pl.ds(pl.multiple_of(t * TILE, TILE), TILE)
            rows[:, cols] = dot(place[...], gathered[k][:, :, cols].reshape(total, TILE)).astype(BF16)

        for l in experts:
            gate_in[l][k].wait()
            up_in[l][k].wait()
            here = pl.ds(l * slots, slots)

            @pl.loop(0, units // TILE)
            def _(t):
                cols = pl.ds(pl.multiple_of(t * TILE, TILE), TILE)
                left = rows[here, pl.ds(0, size)]
                gate = dot(left, gate_at(l, k)[:, cols])
                up = dot(left, up_at(l, k)[:, cols])
                if k > 0:
                    gate = gate + gate_acc[here, cols]
                    up = up + up_acc[here, cols]
                if k < 2:
                    gate_acc[here, cols] = gate
                    up_acc[here, cols] = up
                else:
                    act[here, cols] = (gate / (1.0 + jnp.exp(-gate)) * up).astype(BF16)

            if k == 0:
                down_in[l][0].start()
                down_in[l][1].start()
            if k < 2 and l == max(nl - 2, 0):
                forward(k + 1)

    sib_out, ret_out = [], []

    def pass_on(j):
        cols = pl.ds(j * TILE, TILE)
        sib_out[j].wait_recv()
        value = part32[j % 2, c] + sib[j].astype(F32)
        ssend[j] = value.astype(BF16)
        out_ref[:, cols] = psum[:, cols] + (part32[j % 2, c, h] + sib[j, h].astype(F32))
        for d in range(1, half):
            copy = remote(
                ssend.at[j, lax.rem(h + d, half)],
                rrecv.at[j, d - 1],
                ret_send.at[j, d - 1],
                ret_recv.at[j, d - 1],
                peer(2 * lax.rem(h + d, half) + c),
            )
            copy.start()
            ret_out.append((j, d, copy))

    chunks = feats // TILE
    for j in range(chunks):
        k = min(j * TILE // units, 2)
        inside = pl.ds(j * TILE - spans[k][0], TILE)
        for l in experts:
            if j * TILE == spans[k][0]:
                down_in[l][k].wait()
            here = pl.ds(l * slots, slots)
            block[here, :] = dot(act[here, :], down_at(l, k)[:, inside]).astype(BF16)
        both = dot(comb[...], block[...])
        mixed = both[0:total] + both[total : 2 * total]
        for index in range(group):
            one = mixed[index * rc : (index + 1) * rc]
            part32[j % 2, index % 2, index // 2] = one
            part[j, index % 2, index // 2] = one.astype(BF16)
        copy = remote(part.at[j, 1 - c], sib.at[j], sib_send.at[j], sib_recv.at[j], sibling)
        copy.start()
        sib_out.append(copy)
        if j > 0:
            pass_on(j - 1)
    pass_on(chunks - 1)

    for j, d, copy in ret_out:
        cols = pl.ds(j * TILE, TILE)
        copy.wait_recv()
        out_ref[:, cols] = out_ref[:, cols] + rrecv[j, d - 1].astype(F32)

    for copy in meta_out + sib_out + sum(row_out, []) + sum(fwd_out, []):
        copy.wait_send()
    for _, _, copy in part_out + ret_out:
        copy.wait_send()


def body(
    attn_out,
    residual,
    proj_weight,
    norm_gain,
    gate_weight,
    up_weight,
    down_weight,
    routes,
    route_weights,
):
    mp = lax.axis_size("mp")
    ex = lax.axis_size("expert")
    rc, feats = residual.shape
    nl, _, units = gate_weight.shape
    depth = proj_weight.shape[0]
    group, half = mp * ex, mp * ex // 2
    total, slots = group * rc, nl * group * MOST
    wide, chunks = feats // WIDE, feats // TILE
    rest = feats - 2 * units
    vmem = pl.BlockSpec(memory_space=pltpu.VMEM)
    hbm = pl.BlockSpec(memory_space=pl.ANY)
    dma = pltpu.SemaphoreType.DMA
    added = pl.pallas_call(
        functools.partial(kernel, (mp, ex, rc, nl)),
        out_shape=jax.ShapeDtypeStruct((rc, feats), F32),
        in_specs=[hbm, hbm, hbm, vmem, hbm, hbm, hbm, vmem, vmem],
        out_specs=vmem,
        scratch_shapes=[
            pltpu.VMEM((mp * rc, depth), BF16),
            pltpu.VMEM((rc, feats), F32),
            pltpu.VMEM((nl, 2, units, units), BF16),
            pltpu.VMEM((nl, 2, units, units), BF16),
            pltpu.VMEM((nl, rest, units), BF16),
            pltpu.VMEM((nl, rest, units), BF16),
            pltpu.VMEM((nl, units, rest), BF16),
            pltpu.VMEM((depth, feats), BF16),
            pltpu.VMEM((wide, mp - 1, rc, WIDE), BF16),
            pltpu.VMEM((wide, mp - 1, rc, WIDE), BF16),
            pltpu.VMEM((rc, feats), F32),
            pltpu.VMEM((group, rc, units), BF16),
            pltpu.VMEM((group, rc, units), BF16),
            pltpu.VMEM((group, rc, rest), BF16),
            pltpu.VMEM((group, 8, LANES), F32),
            pltpu.VMEM((slots, total), BF16),
            pltpu.VMEM((2 * total, slots), BF16),
            pltpu.VMEM((slots, units), BF16),
            pltpu.VMEM((slots, units), F32),
            pltpu.VMEM((slots, units), F32),
            pltpu.VMEM((slots, units), BF16),
            pltpu.VMEM((slots, TILE), BF16),
            pltpu.VMEM((2, 2, half, rc, TILE), F32),
            pltpu.VMEM((chunks, 2, half, rc, TILE), BF16),
            pltpu.VMEM((chunks, half, rc, TILE), BF16),
            pltpu.VMEM((chunks, half, rc, TILE), BF16),
            pltpu.VMEM((chunks, half - 1, rc, TILE), BF16),
            dma((mp,)),
            dma(()),
            dma((wide,)),
            dma((nl, 3)),
            dma((nl, 3)),
            dma((nl, 3)),
            dma((group - 1,)),
            dma((group - 1,)),
            dma((wide, mp - 1)),
            dma((wide, mp - 1)),
            dma((3, half - 1)),
            dma((3, half - 1)),
            dma((3, half)),
            dma((3, half)),
            dma((chunks,)),
            dma((chunks,)),
            dma((chunks, half - 1)),
            dma((chunks, half - 1)),
        ],
        compiler_params=pltpu.CompilerParams(
            collective_id=0, has_side_effects=True, vmem_limit_bytes=62 * 1024 * 1024
        ),
    )(
        attn_out,
        residual,
        proj_weight,
        norm_gain,
        gate_weight,
        up_weight,
        down_weight,
        routes.T,
        route_weights.T,
    )
    return added + residual


def solution(mesh):
    in_specs = (
        P("dp", "mp"),
        P(("dp", "mp", "expert"), None),
        P("mp", None),
        P(),
        P("mp", None, "expert"),
        P("mp", None, "expert"),
        P("mp", "expert", None),
        P(("dp", "mp", "expert"), None),
        P(("dp", "mp", "expert"), None),
    )
    out_specs = P(("dp", "mp", "expert"), None)
    return jax.shard_map(body, mesh=mesh, in_specs=in_specs, out_specs=out_specs, check_vma=False)
```

time: 49.9 us -> 52.5 us (1.052)
  Pallas kernels: 44.9 us -> 50.6 us
  local copies, waits for them, and re-layouts: 3.33 us -> 0.01 us
    pallas_call x1, Pallas kernels: 44.9 us -> 50.6 us  [body(): pl.pallas_call(functools.partial(kernel, (mp, ex, rc, nl)), out_shape=jax...]
    add x0 -> x1, other arithmetic: none -> 1.71 us  [body(): return added + residual]
    unnamed x3 -> x2, local copies, waits for them, and re-layouts: 1.7 us -> 0.01 us
    reshape x1 -> x0, local copies, waits for them, and re-layouts: 1.31 us -> none  [body(): norm_gain.reshape(1, feats)]
    transpose x1 -> x0, other arithmetic: 0.69 us -> none  [body(): pairs = jnp.concatenate([routes.astype(F32), route_weights], axis=1).T]
    convert_element_type x1 -> x0, other arithmetic: 0.68 us -> none  [body(): pairs = jnp.concatenate([routes.astype(F32), route_weights], axis=1).T]
where the time goes in v2:
time: 52.5 us; the launch traced here: 52.3 us
  Pallas kernels  50.6 us (96%)
  other arithmetic  1.71 us (3%)
    pallas_call x1, Pallas kernels, body(): pl.pallas_call(functools.partial(kernel, (mp, ex, rc, nl)), out_shape=jax...  50.6 us
    add x1, other arithmetic, body(): return added + residual  1.71 us

profile of v2, /device:TPU:0, one launch (start us, length us, event | category | flops | bytes accessed | tf_op | source)
XLA Modules:
  0.0 52.3 jit_solution(3262856049485541808)
XLA Ops:
  0.0 0.0 copy-start
  0.0 50.6 %shard_map.91 = f32[32,2304]{1,0:T(8,128)} custom-call(bf16[256,1152]{1,0:T(8,128)(2,1)} %attn_ref.1, f32[32,2304]{1,0:T(8,128)} %residual_ref.1, bf16[1152,2304]{1,0:T(8,128)(2,1)} %proj_ref.1, f32[2304]{0:T(1024)} %gain_ref.1, bf16[4,2304,1024]{2,1,0:T(8,128)(2,1)} %gate_ref.1, bf16[4,2304,1024]{2,1,0:T(8,128)(2,1)} %up_ref.1, ...), custom_call_target="tpu_custom_call" | custom-call | tf_op jit(solution)/shard_map/pallas_call | solution.py:393
  50.6 0.0 copy-done
  50.6 1.7 %add.3 = f32[32,2304]{1,0:T(8,128)} add(f32[32,2304]{1,0:T(8,128)} %shard_map.91, f32[32,2304]{1,0:T(8,128)S(1)} %copy-done) | non-fusion elementwise | flops 73728 | bytes 884736 | tf_op jit(solution)/shard_map/add | solution.py:459
Async XLA Ops:
  0.0 50.6 %copy-start = (f32[32,2304]{1,0:T(8,128)S(1)}, f32[32,2304]{1,0:T(8,128)}, u32[]{:S(2)}) copy-start(f32[32,2304]{1,0:T(8,128)} %residual_ref.1) | copy-start | bytes 884740

commit v3 on v2

--- a/solution.py
+++ b/solution.py
@@ -12,6 +12,7 @@
 LANES = 128
 TILE = 256
 WIDE = 768
+LAG = 3
 MESH = pl.DeviceIdType.MESH
 BF16 = jnp.bfloat16
 F32 = jnp.float32
@@ -280,90 +281,124 @@
             fwd_out[k][d].start()
 
     forward(0)
-    for k, (start, size) in enumerate(spans):
+
+    def dispatch(k, at):
         for copy in fwd_out[k]:
             copy.wait_recv()
 
+        @pl.loop(0, spans[k][1] // TILE)
+        def _(t):
+            cols = pl.ds(pl.multiple_of(t * TILE, TILE), TILE)
+            to = pl.ds(pl.multiple_of(at + t * TILE, TILE), TILE)
+            rows[:, to] = dot(place[...], gathered[k][:, :, cols].reshape(total, TILE)).astype(BF16)
+
+    dispatch(0, 0)
+    for l in experts:
+        gate_in[l][0].wait()
+        up_in[l][0].wait()
+        here = pl.ds(l * slots, slots)
+
+        @pl.loop(0, units // TILE)
+        def _(t):
+            cols = pl.ds(pl.multiple_of(t * TILE, TILE), TILE)
+            left = rows[here, pl.ds(0, units)]
+            gate_acc[here, cols] = dot(left, gate_big[l, 0, :, cols])
+            up_acc[here, cols] = dot(left, up_big[l, 0, :, cols])
+
+        down_in[l][0].start()
+        down_in[l][1].start()
+        if l == max(nl - 2, 0):
+            forward(1)
+            forward(2)
+
+    dispatch(1, 0)
+    dispatch(2, units)
+    for l in experts:
+        for k in (1, 2):
+            gate_in[l][k].wait()
+            up_in[l][k].wait()
+        here = pl.ds(l * slots, slots)
+
+        @pl.loop(0, units // TILE)
+        def _(t):
+            cols = pl.ds(pl.multiple_of(t * TILE, TILE), TILE)
+            left = rows[here, pl.ds(0, units)]
+            last = rows[here, pl.ds(units, rest)]
+            gate = dot(left, gate_big[l, 1, :, cols]) + dot(last, gate_small[l, :, cols])
+            up = dot(left, up_big[l, 1, :, cols]) + dot(last, up_small[l, :, cols])
+            gate = gate + gate_acc[here, cols]
+            up = up + up_acc[here, cols]
+            act[here, cols] = (gate / (1.0 + jnp.exp(-gate)) * up).astype(BF16)
+
+    def to_sibling(j):
+        return remote(part.at[j, 1 - c], sib.at[j], sib_send.at[j], sib_recv.at[j], sibling)
+
+    def to_owner(j, d):
+        return remote(
+            ssend.at[j, lax.rem(h + d, half)],
+            rrecv.at[j, d - 1],
+            ret_send.at[j, d - 1],
+            ret_recv.at[j, d - 1],
+            peer(2 * lax.rem(h + d, half) + c),
+        )
+
+    def columns(j):
+        return pl.ds(pl.multiple_of(j * TILE, TILE), TILE)
+
+    def pass_on(j):
+        to_sibling(j).wait_recv()
+        slot = lax.rem(j, LAG + 1)
+        ssend[j] = (part32[slot, c] + sib[j].astype(F32)).astype(BF16)
+        for d in range(1, half):
+            to_owner(j, d).start()
+        own = part32[slot, c, h] + sib[j, h].astype(F32)
+        out_ref[:, columns(j)] = psum[:, columns(j)] + own
+
+    chunks = feats // TILE
+    for k, (start, size) in enumerate(spans):
+        for l in experts:
+            down_in[l][k].wait()
+
         @pl.loop(0, size // TILE)
         def _(t):
-            cols = pl.ds(pl.multiple_of(t * TILE, TILE), TILE)
-            rows[:, cols] = dot(place[...], gathered[k][:, :, cols].reshape(total, TILE)).astype(BF16)
-
-        for l in experts:
-            gate_in[l][k].wait()
-            up_in[l][k].wait()
-            here = pl.ds(l * slots, slots)
-
-            @pl.loop(0, units // TILE)
-            def _(t):
-                cols = pl.ds(pl.multiple_of(t * TILE, TILE), TILE)
-                left = rows[here, pl.ds(0, size)]
-                gate = dot(left, gate_at(l, k)[:, cols])
-                up = dot(left, up_at(l, k)[:, cols])
-                if k > 0:
-                    gate = gate + gate_acc[here, cols]
-                    up = up + up_acc[here, cols]
-                if k < 2:
-                    gate_acc[here, cols] = gate
-                    up_acc[here, cols] = up
-                else:
-                    act[here, cols] = (gate / (1.0 + jnp.exp(-gate)) * up).astype(BF16)
-
-            if k == 0:
-                down_in[l][0].start()
-                down_in[l][1].start()
-            if k < 2 and l == max(nl - 2, 0):
-                forward(k + 1)
-
-    sib_out, ret_out = [], []
-
-    def pass_on(j):
-        cols = pl.ds(j * TILE, TILE)
-        sib_out[j].wait_recv()
-        value = part32[j % 2, c] + sib[j].astype(F32)
-        ssend[j] = value.astype(BF16)
-        out_ref[:, cols] = psum[:, cols] + (part32[j % 2, c, h] + sib[j, h].astype(F32))
+            j = start // TILE + t
+            for l in experts:
+                here = pl.ds(l * slots, slots)
+                block[here, :] = dot(act[here, :], down_at(l, k)[:, columns(t)]).astype(BF16)
+            both = dot(comb[...], block[...])
+            mixed = both[0:total] + both[total : 2 * total]
+            slot = lax.rem(j, LAG + 1)
+            for index in range(group):
+                one = mixed[index * rc : (index + 1) * rc]
+                part32[slot, index % 2, index // 2] = one
+                part[j, index % 2, index // 2] = one.astype(BF16)
+            to_sibling(j).start()
+
+            @pl.when(j >= LAG)
+            def _():
+                pass_on(j - LAG)
+
+    @pl.loop(chunks - LAG, chunks)
+    def _(j):
+        pass_on(j)
+
+    @pl.loop(0, chunks)
+    def _(j):
+        value = out_ref[:, columns(j)]
         for d in range(1, half):
-            copy = remote(
-                ssend.at[j, lax.rem(h + d, half)],
-                rrecv.at[j, d - 1],
-                ret_send.at[j, d - 1],
-                ret_recv.at[j, d - 1],
-                peer(2 * lax.rem(h + d, half) + c),
-            )
-            copy.start()
-            ret_out.append((j, d, copy))
-
-    chunks = feats // TILE
-    for j in range(chunks):
-        k = min(j * TILE // units, 2)
-        inside = pl.ds(j * TILE - spans[k][0], TILE)
-        for l in experts:
-            if j * TILE == spans[k][0]:
-                down_in[l][k].wait()
-            here = pl.ds(l * slots, slots)
-            block[here, :] = dot(act[here, :], down_at(l, k)[:, inside]).astype(BF16)
-        both = dot(comb[...], block[...])
-        mixed = both[0:total] + both[total : 2 * total]
-        for index in range(group):
-            one = mixed[index * rc : (index + 1) * rc]
-            part32[j % 2, index % 2, index // 2] = one
-            part[j, index % 2, index // 2] = one.astype(BF16)
-        copy = remote(part.at[j, 1 - c], sib.at[j], sib_send.at[j], sib_recv.at[j], sibling)
-        copy.start()
-        sib_out.append(copy)
-        if j > 0:
-            pass_on(j - 1)
-    pass_on(chunks - 1)
-
-    for j, d, copy in ret_out:
-        cols = pl.ds(j * TILE, TILE)
-        copy.wait_recv()
-        out_ref[:, cols] = out_ref[:, cols] + rrecv[j, d - 1].astype(F32)
-
-    for copy in meta_out + sib_out + sum(row_out, []) + sum(fwd_out, []):
+            to_owner(j, d).wait_recv()
+            value = value + rrecv[j, d - 1].astype(F32)
+        out_ref[:, columns(j)] = value
+
+    @pl.loop(0, chunks)
+    def _(j):
+        to_sibling(j).wait_send()
+        for d in range(1, half):
+            to_owner(j, d).wait_send()
+
+    for copy in meta_out + sum(row_out, []) + sum(fwd_out, []):
         copy.wait_send()
-    for _, _, copy in part_out + ret_out:
+    for _, _, copy in part_out:
         copy.wait_send()
 
 
@@ -413,12 +448,12 @@
             pltpu.VMEM((group, 8, LANES), F32),
             pltpu.VMEM((slots, total), BF16),
             pltpu.VMEM((2 * total, slots), BF16),
-            pltpu.VMEM((slots, units), BF16),
+            pltpu.VMEM((slots, units + rest), BF16),
             pltpu.VMEM((slots, units), F32),
             pltpu.VMEM((slots, units), F32),
             pltpu.VMEM((slots, units), BF16),
             pltpu.VMEM((slots, TILE), BF16),
-            pltpu.VMEM((2, 2, half, rc, TILE), F32),
+            pltpu.VMEM((LAG + 1, 2, half, rc, TILE), F32),
             pltpu.VMEM((chunks, 2, half, rc, TILE), BF16),
             pltpu.VMEM((chunks, half, rc, TILE), BF16),
             pltpu.VMEM((chunks, half, rc, TILE), BF16),

time: 52.5 us -> 48.1 us (0.916)
  Pallas kernels: 50.6 us -> 46.2 us
    pallas_call x1, Pallas kernels: 50.6 us -> 46.2 us  [body(): pl.pallas_call(functools.partial(kernel, (mp, ex, rc, nl)), out_shape=jax...]
where the time goes in v3:
time: 48.1 us; the launch traced here: 48 us
  Pallas kernels  46.2 us (96%)
  other arithmetic  1.71 us (4%)
    pallas_call x1, Pallas kernels, body(): pl.pallas_call(functools.partial(kernel, (mp, ex, rc, nl)), out_shape=jax...  46.2 us
    add x1, other arithmetic, body(): return added + residual  1.71 us

profile of v3, /device:TPU:0, one launch (start us, length us, event | category | flops | bytes accessed | tf_op | source)
XLA Modules:
  0.0 48.0 jit_solution(10181348732769837069)
XLA Ops:
  0.0 0.0 copy-start
  0.0 46.2 %shard_map.91 = f32[32,2304]{1,0:T(8,128)} custom-call(bf16[256,1152]{1,0:T(8,128)(2,1)} %attn_ref.1, f32[32,2304]{1,0:T(8,128)} %residual_ref.1, bf16[1152,2304]{1,0:T(8,128)(2,1)} %proj_ref.1, f32[2304]{0:T(1024)} %gain_ref.1, bf16[4,2304,1024]{2,1,0:T(8,128)(2,1)} %gate_ref.1, bf16[4,2304,1024]{2,1,0:T(8,128)(2,1)} %up_ref.1, ...), custom_call_target="tpu_custom_call" | custom-call | tf_op jit(solution)/shard_map/pallas_call | solution.py:428
  46.3 0.0 copy-done
  46.3 1.7 %add.3 = f32[32,2304]{1,0:T(8,128)} add(f32[32,2304]{1,0:T(8,128)} %shard_map.91, f32[32,2304]{1,0:T(8,128)S(1)} %copy-done) | non-fusion elementwise | flops 73728 | bytes 884736 | tf_op jit(solution)/shard_map/add | solution.py:494
Async XLA Ops:
  0.0 46.3 %copy-start = (f32[32,2304]{1,0:T(8,128)S(1)}, f32[32,2304]{1,0:T(8,128)}, u32[]{:S(2)}) copy-start(f32[32,2304]{1,0:T(8,128)} %residual_ref.1) | copy-start | bytes 884740
